TPU v7x, 128 devices: a whole 4x4x4 slice. The times are simulated.
128 devices in a mesh: ep: 16 (over z, x), etp: 8 (over y, core).
Axes of the slice: x: 4, y: 4, z: 4, core: 2. Of those that a mesh axis runs over, the one named last changes fastest.
Arguments:
- tokens: bfloat16 [2048, 3072], P('ep', 'etp'), may hold values from -6 to 6
- grad_out: bfloat16 [2048, 3072], P('ep', 'etp'), may hold values from -6 to 6
- probs: float32 [2048, 4], P('ep'), may hold values from 0.1 to 1
- expert_ids: int32 [2048, 4], P('ep'), may hold values from 0 to 15, all different within a row; in each aligned block of 128 rows (0 to 127, 128 to 255, ...) at most 48 rows name the same one
- w_gate: bfloat16 [16, 3072, 5376], P('ep', None, 'etp'), may hold values from -0.109375 to 0.109375
- w_up: bfloat16 [16, 3072, 5376], P('ep', None, 'etp'), may hold values from -0.109375 to 0.109375
- w_down: bfloat16 [16, 5376, 3072], P('ep', 'etp'), may hold values from -0.078125 to 0.078125
Outputs:
- grad_tokens: bfloat16 [2048, 3072], P('ep', 'etp')
- grad_gate: bfloat16 [16, 3072, 5376], P('ep', None, 'etp')
- grad_up: bfloat16 [16, 3072, 5376], P('ep', None, 'etp')
- grad_down: bfloat16 [16, 5376, 3072], P('ep', 'etp')
Inputs may be any that keep to these rules, and one draw needn't show every extreme that they name: `expert_ids`: each row names 4 different experts. In the rows of one index of ep (aligned blocks of 128 rows) no expert is named by more than 48 rows, a bound that some block reaches.
All inputs are finite; a program needn't handle non-finite values.
Results may differ from a plain program's by a relative error of at most 0.02.
Values may be sent and summed in bfloat16 or wider, within the bound.
A program may use at most 128 MiB of HBM per device.

v0:
```python
import functools
import jax
import jax.numpy as jnp
from jax import lax
from jax.experimental import pallas as pl
from jax.experimental.pallas import tpu as pltpu
from jax.sharding import PartitionSpec as P

BF = jnp.bfloat16
F32 = jnp.float32
CAP = 48
SLOTS = 16
ROWS = CAP * SLOTS
GROUP = 4
GROWS = GROUP * CAP
CHUNKS = ((0, 2), (2, 4))
MESH = pl.DeviceIdType.MESH


def nt(a, b):
    return lax.dot_general(a, b, (((1,), (1,)), ((), ())), preferred_element_type=F32)


def tn(a, b):
    return lax.dot_general(a, b, (((0,), (0,)), ((), ())), preferred_element_type=F32)


def nn(a, b):
    return jnp.dot(a, b, preferred_element_type=F32)


def expert_kernel(
    tokens, gout, ids, probs, wg_h, wu_h, wd_h,
    gt_out, gg_h, gu_h, gd_h,
    xg, snd, raw, wg, wu, wd, place, pw,
    hid, gpg, gpu, acc_g, acc_u, acc_h,
    part, from_sib, from_y, snd_back, back, tail_snd, tail_rcv, stage_g, stage_d,
    sem_w, sem_raw, sem_self, sem_send, sem_recv, sem_fsend, sem_frecv,
    sem_psend, sem_precv, sem_ysend, sem_yrecv, sem_bself, sem_bsend, sem_brecv, sem_tail, sem_out,
):
    ep = lax.axis_index("ep")
    t = lax.axis_index("etp")
    z, x = ep // 4, ep % 4
    y, core = t // 2, t % 2
    width = tokens.shape[1]
    t_up, t_down, t_far = (t + 2) % 8, (t + 6) % 8, (t + 4) % 8
    t_sib = t + 1 - 2 * core

    def target(j):
        i = j % 4
        return ((z + i) % 4) * 4 + (x + i + j // 4) % 4

    def source(j):
        i = j % 4
        return ((z + 4 - i) % 4) * 4 + (x + 8 - i - j // 4) % 4

    def cols(f):
        return pl.ds(pl.multiple_of(f * width, 128), width)

    def slot(j):
        return pl.ds(pl.multiple_of(j * CAP, 16), CAP)

    def remote(src, dst, ss, rs, e, f):
        return pltpu.make_async_remote_copy(
            src_ref=src, dst_ref=dst, send_sem=ss, recv_sem=rs,
            device_id={"ep": e, "etp": f}, device_id_type=MESH,
        )

    w_copies = [
        pltpu.make_async_copy(h.at[0], v, sem_w.at[i])
        for i, (h, v) in enumerate(((wg_h, wg), (wu_h, wu), (wd_h, wd)))
    ]
    for copy in w_copies:
        copy.start()

    barrier = pltpu.get_barrier_semaphore()

    @pl.loop(1, SLOTS)
    def _(j):
        pl.semaphore_signal(barrier, inc=1, device_id={"ep": target(j), "etp": t}, device_id_type=MESH)

    for f in (t_up, t_down, t_far, t_sib):
        pl.semaphore_signal(barrier, inc=1, device_id={"ep": ep, "etp": f}, device_id_type=MESH)

    lane = lax.broadcasted_iota(jnp.int32, (128, 128), 1)
    row = lax.broadcasted_iota(jnp.int32, (128, 128), 0)
    li = lane & 3
    expert = ((z + li) & 3) * 4 + ((x + li + (lane >> 2)) & 3)
    expert = jnp.where(lane < SLOTS, expert, -1)
    hit = jnp.zeros((128, 128), F32)
    weight = jnp.zeros((128, 128), F32)
    for k in range(ids.shape[1]):
        same = ids[:, k : k + 1] == expert
        hit = hit + jnp.where(same, 1.0, 0.0)
        weight = weight + jnp.where(same, probs[:, k : k + 1], 0.0)
    hit = hit.T[:SLOTS]
    weight = weight.T[:SLOTS]
    earlier = jnp.where(row < lane, 1.0, 0.0).astype(BF)
    pos = nn(hit.astype(BF), earlier)
    rank = lax.broadcasted_iota(jnp.int32, (CAP, 128), 0).astype(F32)
    for j in range(SLOTS):
        one = jnp.where(pos[j : j + 1] == rank, hit[j : j + 1], 0.0)
        place[j * CAP : (j + 1) * CAP, :] = one.astype(BF)
        pw[j * CAP : (j + 1) * CAP, :] = jnp.broadcast_to(
            jnp.sum(one * weight[j : j + 1], axis=1, keepdims=True), (CAP, 128)
        )

    pl.semaphore_wait(barrier, SLOTS - 1 + 4)

    raw_copies = [
        remote(src, raw.at[i], sem_raw.at[0, i], sem_raw.at[1, i], ep, t_far)
        for i, src in enumerate((tokens, gout))
    ]
    for copy in raw_copies:
        copy.start()

    def fill(b, g, tok, grad):
        rows = pl.ds(g * GROWS, GROWS)
        one = place[rows, :]
        snd[b, 0, rows, :] = nn(one, tok).astype(BF)
        snd[b, 1, rows, :] = (nn(one, grad) * pw[rows, 0:1]).astype(BF)

    def own_copy(b):
        f = (t, t_far)[b]
        return pltpu.make_async_copy(
            snd.at[b, :, pl.ds(0, CAP), :], xg.at[:, pl.ds(0, CAP), cols(f)], sem_self.at[b]
        )

    def out_copy(b, j, e):
        f = (t, t_far)[b]
        return remote(
            snd.at[b, :, slot(j), :], xg.at[:, slot(j), cols(f)],
            sem_send.at[b, j], sem_recv.at[b, j], e, t,
        )

    def send(b, g):
        if g == 0:
            own_copy(b).start()

        @pl.loop(max(1, g * GROUP), (g + 1) * GROUP)
        def _(j):
            out_copy(b, j, target(j)).start()

    def fwd_copy(kind, g):
        rows = pl.ds(g * GROWS, GROWS)
        f = (t, t, t, t_far, t_down, t_up)[kind]
        to = (t_up, t_down, t_sib, t_sib, t_sib, t_sib)[kind]
        ref = xg.at[:, rows, cols(f)]
        return remote(ref, ref, sem_fsend.at[kind, g], sem_frecv.at[kind, g], ep, to)

    def arrived(kind, g):
        rows = pl.ds(g * GROWS, GROWS)
        f = (t_down, t_up, t_sib, (t_sib + 4) % 8, (t_sib + 6) % 8, (t_sib + 2) % 8)[kind]
        ref = xg.at[:, rows, cols(f)]
        return remote(ref, ref, sem_fsend.at[kind, g], sem_frecv.at[kind, g], ep, t_sib)

    def got(b, g):
        if g == 0:
            own_copy(b).wait()

        @pl.loop(max(1, g * GROUP), (g + 1) * GROUP)
        def _(j):
            out_copy(b, j, source(j)).wait_recv()

    def fwd_a(g):
        got(0, g)
        for kind in (0, 1, 2):
            fwd_copy(kind, g).start()

    def fwd_b(g):
        got(1, g)
        fwd_copy(3, g).start()

    def fwd_y(g):
        for kind in (0, 1):
            arrived(kind, g).wait_recv()
            fwd_copy(4 + kind, g).start()

    def whole(g):
        for kind in (2, 3, 4, 5):
            arrived(kind, g).wait_recv()

    for g in range(4):
        fill(0, g, tokens[...], gout[...])
        send(0, g)
        if g == 1:
            for copy in raw_copies:
                copy.wait_recv()
        if g >= 1:
            fill(1, g - 1, raw[0], raw[1])
            send(1, g - 1)
    fill(1, 3, raw[0], raw[1])
    send(1, 3)

    def tiles(n, body, services=None):
        services = services or {}

        @pl.loop(0, n)
        def _(k):
            body(k)
            for at, calls in services.items():
                @pl.when(k == at)
                def _():
                    for call in calls:
                        call()

    def forward(c, services=None):
        g0, g1 = CHUNKS[c]
        n = (g1 - g0) * GROWS
        rows = pl.ds(g0 * GROWS, n)
        top = pl.ds(0, n)
        tile = 512

        def body(k):
            ks = pl.ds(pl.multiple_of(k * tile, tile), tile)
            xk = xg[0, rows, ks]
            gk = xg[1, rows, ks]
            g = nn(xk, wg[ks, :])
            u = nn(xk, wu[ks, :])
            h = nt(gk, wd[:, ks])

            @pl.when(k == 0)
            def _():
                acc_g[top, :] = g
                acc_u[top, :] = u
                acc_h[top, :] = h

            @pl.when(k > 0)
            def _():
                acc_g[top, :] += g
                acc_u[top, :] += u
                acc_h[top, :] += h

        tiles(xg.shape[2] // tile, body, services)
        piece = 96

        @pl.loop(0, n // piece)
        def _(i):
            rs = pl.ds(pl.multiple_of(i * piece, piece), piece)
            rd = pl.ds(pl.multiple_of(g0 * GROWS + i * piece, 16), piece)
            g = acc_g[rs, :]
            u = acc_u[rs, :]
            h = acc_h[rs, :]
            s = jax.nn.sigmoid(g)
            sg = g * s
            hid[rd, :] = (sg * u).astype(BF)
            gpg[rd, :] = (h * u * s * (1.0 + g * (1.0 - s))).astype(BF)
            gpu[rd, :] = (h * sg).astype(BF)

    steps = (1, 3, 2, 0)

    def chunk_rows(c):
        g0, g1 = CHUNKS[c]
        return pl.ds(g0 * GROWS, (g1 - g0) * GROWS)

    def sib_copy(c, i):
        rows = chunk_rows(c)
        return remote(
            part.at[i, 1 - core, rows, :], from_sib.at[i, rows, :],
            sem_psend.at[c, i], sem_precv.at[c, i], ep, t_sib,
        )

    def y_copy(c, i):
        rows = chunk_rows(c)
        return remote(
            part.at[i, core, rows, :], from_y.at[i, rows, :],
            sem_ysend.at[c, i], sem_yrecv.at[c, i], ep, (t_up, t_down)[i],
        )

    def quarter(c, i):
        rows = chunk_rows(c)
        q = (y + steps[i]) % 4
        ws = pl.ds(pl.multiple_of(q * 2 * width, 128), 2 * width)
        p = nt(gpg[rows, :], wg[ws, :]) + nt(gpu[rows, :], wu[ws, :])
        part[i, 0, rows, :] = p[:, :width].astype(BF)
        part[i, 1, rows, :] = p[:, width:].astype(BF)
        sib_copy(c, i).start()

    def pair(c, i):
        rows = chunk_rows(c)
        sib_copy(c, i).wait_recv()
        return part[i, core, rows, :].astype(F32) + from_sib[i, rows, :].astype(F32)

    def pair_y(c, i):
        part[i, core, chunk_rows(c), :] = pair(c, i).astype(BF)
        y_copy(c, i).start()

    def back_copy(b, j, e):
        return remote(
            snd_back.at[b, slot(j), :], back.at[b, slot(j), :],
            sem_bsend.at[b, j], sem_brecv.at[b, j], e, t,
        )

    def own_back(b):
        return pltpu.make_async_copy(
            snd_back.at[b, pl.ds(0, CAP), :], back.at[b, pl.ds(0, CAP), :], sem_bself.at[b]
        )

    def send_back(c, b):
        g0, g1 = CHUNKS[c]
        if g0 == 0:
            own_back(b).start()

        @pl.loop(max(1, g0 * GROUP), g1 * GROUP)
        def _(j):
            back_copy(b, j, source(j)).start()

    def pair_far(c):
        snd_back[1, chunk_rows(c), :] = pair(c, 2).astype(BF)
        send_back(c, 1)

    def pair_own(c):
        rows = chunk_rows(c)
        mine = pair(c, 3)
        for i in (0, 1):
            y_copy(c, i).wait_recv()
            mine = mine + from_y[i, rows, :].astype(F32)
        snd_back[0, rows, :] = mine.astype(BF)
        send_back(c, 0)

    tail = remote(tail_snd, tail_rcv, sem_tail.at[0], sem_tail.at[1], ep, t_far)

    def got_back(b):
        own_back(b).wait()

        @pl.loop(1, SLOTS)
        def _(j):
            back_copy(b, j, target(j)).wait_recv()

    def combine_far():
        got_back(1)
        tail_snd[...] = tn(place[...], back[1]).astype(BF)
        tail.start()

    def combine_own():
        got_back(0)
        mine = tn(place[...], back[0])
        tail.wait_recv()
        gt_out[...] = (mine + tail_rcv[...].astype(F32)).astype(BF)

    wt = 512

    def down_copy(k):
        ks = pl.ds(pl.multiple_of(k * wt, wt), wt)
        return pltpu.make_async_copy(stage_d.at[k % 2], gd_h.at[0, :, ks], sem_out.at[0, k % 2])

    def gate_copy(k, i):
        ks = pl.ds(pl.multiple_of(k * wt, wt), wt)
        return pltpu.make_async_copy(stage_g.at[i, k % 2], (gg_h, gu_h)[i].at[0, ks, :], sem_out.at[1 + i, k % 2])

    def down_tile(k):
        ks = pl.ds(pl.multiple_of(k * wt, wt), wt)

        @pl.when(k >= 2)
        def _():
            down_copy(k - 2).wait()

        stage_d[k % 2] = tn(hid[...], xg[1, :, ks]).astype(BF)
        down_copy(k).start()

    def gate_tile(k):
        ks = pl.ds(pl.multiple_of(k * wt, wt), wt)
        for i in (0, 1):
            @pl.when(k >= 2)
            def _():
                gate_copy(k - 2, i).wait()

            stage_g[i, k % 2] = tn(xg[0, :, ks], (gpg, gpu)[i][...]).astype(BF)
            gate_copy(k, i).start()

    nw = xg.shape[2] // wt

    fwd_a(0)
    fwd_a(1)
    fwd_b(0)
    fwd_y(0)
    fwd_b(1)
    fwd_a(2)
    fwd_y(1)
    for copy in w_copies:
        copy.wait()
    whole(0)
    whole(1)
    forward(0, {
        0: [lambda: fwd_b(2)], 1: [lambda: fwd_a(3)], 2: [lambda: fwd_y(2)],
        3: [lambda: fwd_b(3)], 5: [lambda: fwd_y(3)],
    })
    quarter(0, 0)
    quarter(0, 1)
    pair_y(0, 0)
    quarter(0, 2)
    pair_y(0, 1)
    quarter(0, 3)
    pair_far(0)
    whole(2)
    whole(3)
    forward(1, {1: [lambda: pair_own(0)]})
    quarter(1, 0)
    quarter(1, 1)
    pair_y(1, 0)
    quarter(1, 2)
    pair_y(1, 1)
    quarter(1, 3)
    pair_far(1)
    tiles(nw, down_tile, {2: [lambda: pair_own(1)]})
    tiles(nw, gate_tile, {2: [combine_far], 4: [combine_own]})

    for k in (nw - 2, nw - 1):
        down_copy(k).wait()
        for i in (0, 1):
            gate_copy(k, i).wait()
    for copy in raw_copies:
        copy.wait_send()
    tail.wait_send()
    for b in (0, 1):
        @pl.loop(1, SLOTS)
        def _(j):
            out_copy(b, j, target(j)).wait_send()
            back_copy(b, j, source(j)).wait_send()

    for g in range(4):
        for kind in range(6):
            fwd_copy(kind, g).wait_send()
    for c in range(len(CHUNKS)):
        for i in range(4):
            sib_copy(c, i).wait_send()
        for i in range(2):
            y_copy(c, i).wait_send()


def local(tokens, grad_out, probs, expert_ids, w_gate, w_up, w_down):
    toks, width = tokens.shape
    _, d, ff = w_gate.shape
    vmem = pl.BlockSpec(memory_space=pltpu.VMEM)
    hbm = pl.BlockSpec(memory_space=pl.ANY)
    dma = pltpu.SemaphoreType.DMA
    n = max(b - a for a, b in CHUNKS) * GROWS
    nc = len(CHUNKS)
    gt, gg, gu, gd = pl.pallas_call(
        expert_kernel,
        out_shape=[
            jax.ShapeDtypeStruct((toks, width), BF),
            jax.ShapeDtypeStruct(w_gate.shape, BF),
            jax.ShapeDtypeStruct(w_up.shape, BF),
            jax.ShapeDtypeStruct(w_down.shape, BF),
        ],
        in_specs=[vmem] * 4 + [hbm] * 3,
        out_specs=[vmem] + [hbm] * 3,
        scratch_shapes=[
            pltpu.VMEM((2, ROWS, d), BF),
            pltpu.VMEM((2, 2, ROWS, width), BF),
            pltpu.VMEM((2, toks, width), BF),
            pltpu.VMEM((d, ff), BF),
            pltpu.VMEM((d, ff), BF),
            pltpu.VMEM((ff, d), BF),
            pltpu.VMEM((ROWS, toks), BF),
            pltpu.VMEM((ROWS, 128), F32),
            pltpu.VMEM((ROWS, ff), BF),
            pltpu.VMEM((ROWS, ff), BF),
            pltpu.VMEM((ROWS, ff), BF),
            pltpu.VMEM((n, ff), F32),
            pltpu.VMEM((n, ff), F32),
            pltpu.VMEM((n, ff), F32),
            pltpu.VMEM((4, 2, ROWS, width), BF),
            pltpu.VMEM((4, ROWS, width), BF),
            pltpu.VMEM((2, ROWS, width), BF),
            pltpu.VMEM((2, ROWS, width), BF),
            pltpu.VMEM((2, ROWS, width), BF),
            pltpu.VMEM((toks, width), BF),
            pltpu.VMEM((toks, width), BF),
            pltpu.VMEM((2, 2, 512, ff), BF),
            pltpu.VMEM((2, ff, 512), BF),
            dma((3,)),
            dma((2, 2)),
            dma((2,)),
            dma((2, SLOTS)),
            dma((2, SLOTS)),
            dma((6, 4)),
            dma((6, 4)),
            dma((nc, 4)),
            dma((nc, 4)),
            dma((nc, 2)),
            dma((nc, 2)),
            dma((2,)),
            dma((2, SLOTS)),
            dma((2, SLOTS)),
            dma((2,)),
            dma((3, 2)),
        ],
        compiler_params=pltpu.CompilerParams(
            collective_id=0, has_side_effects=True, vmem_limit_bytes=60 * 2**20
        ),
    )(tokens, grad_out, expert_ids, probs, w_gate, w_up, w_down)
    return gt, gg, gu, gd


def solution(mesh):
    return jax.shard_map(
        local,
        mesh=mesh,
        in_specs=(
            P("ep", "etp"),
            P("ep", "etp"),
            P("ep", None),
            P("ep", None),
            P("ep", None, "etp"),
            P("ep", None, "etp"),
            P("ep", "etp", None),
        ),
        out_specs=(
            P("ep", "etp"),
            P("ep", None, "etp"),
            P("ep", None, "etp"),
            P("ep", "etp", None),
        ),
        check_vma=False,
    )
```

profile of v0, /device:TPU:0, one launch (start us, length us, event | category | flops | bytes accessed | tf_op | source)
XLA Modules:
  0.0 134.8 jit_solution(2345422634497306789)
XLA Ops:
  0.6 1.4 %copy.12.probs = f32[128,4]{1,0:T(8,128)} copy(f32[128,4]{0,1:T(4,128)} %param.9) | data formatting | bytes 4096 | tf_op args[2]
  2.0 1.4 %copy.11.ids = s32[128,4]{1,0:T(8,128)} copy(s32[128,4]{0,1:T(4,128)} %param.10) | data formatting | bytes 4096 | tf_op args[3]
  3.5 6.4 %copy.13.wg_h = bf16[1,3072,672]{2,1,0:T(8,128)(2,1)} copy(bf16[1,3072,672]{1,2,0:T(8,128)(2,1)} %param.11) | data formatting | bytes 8257536 | tf_op args[4]
  9.9 6.5 %copy.14.wu_h = bf16[1,3072,672]{2,1,0:T(8,128)(2,1)} copy(bf16[1,3072,672]{1,2,0:T(8,128)(2,1)} %param.12) | data formatting | bytes 8257536 | tf_op args[5]
  16.4 100.4 %shard_map.102 = (bf16[128,384]{1,0:T(8,128)(2,1)}, bf16[1,3072,672]{2,1,0:T(8,128)(2,1)}, bf16[1,3072,672]{2,1,0:T(8,128)(2,1)}, bf16[1,672,3072]{2,1,0:T(8,128)(2,1)}) custom-call(bf16[128,384]{1,0:T(8,128)(2,1)} %tokens.1, bf16[128,384]{1,0:T(8,128)(2,1)} %gout.1, s32[128,4]{1,0:T(8,128)} %copy.11.ids, f32[128,4]{1,0:T(8,128)} %copy.12.probs, ...), custom_call_target="tpu_custom_call" | custom-call | tf_op jit(solution)/shard_map/pallas_call | solution.py:439
  116.8 6.4 %copy.15 = bf16[1,3072,672]{1,2,0:T(8,128)(2,1)} copy(bf16[1,3072,672]{2,1,0:T(8,128)(2,1)} %get-tuple-element.5) | data formatting | bytes 8257536 | tf_op jit(solution)/shard_map/pallas_call | solution.py:439
  123.2 0.0 copy-start
  123.2 6.4 %copy.16 = bf16[1,3072,672]{1,2,0:T(8,128)(2,1)} copy(bf16[1,3072,672]{2,1,0:T(8,128)(2,1)} %get-tuple-element.6) | data formatting | bytes 8257536 | tf_op jit(solution)/shard_map/pallas_call | solution.py:439
  129.7 0.0 copy-done
  129.7 0.6 copy.19
  130.3 4.4 %copy.20 = bf16[1,672,3072]{2,1,0:T(8,128)(2,1)} copy(bf16[1,672,3072]{2,1,0:T(8,128)(2,1)} %get-tuple-element.15) | data formatting | bytes 8257536
Async XLA Ops:
  123.2 6.4 %copy-start = (bf16[128,384]{1,0:T(8,128)(2,1)S(1)}, bf16[128,384]{1,0:T(8,128)(2,1)}, u32[]{:S(2)}) copy-start(bf16[128,384]{1,0:T(8,128)(2,1)} %get-tuple-element.12) | copy-start | bytes 294916
where the time goes:
time: 136 us; the launch traced here: 135 us
  Pallas kernels  100 us (74%)
  local copies, waits for them, and re-layouts  33.7 us (25%)
    pallas_call x1, Pallas kernels, local(): pl.pallas_call(expert_kernel, out_shape=[jax.ShapeDtypeStruct((toks, widt...  100 us
    unnamed x8, local copies, waits for them, and re-layouts  20.9 us
    pallas_call x2, local copies, waits for them, and re-layouts, local(): pl.pallas_call(expert_kernel, out_shape=[jax.ShapeDtypeStruct((toks, widt...  12.9 us

commit v1 on v0

v1 whole, which is shorter than its diff:
```python
import functools
import jax
import jax.numpy as jnp
from jax import lax
from jax.experimental import pallas as pl
from jax.experimental.pallas import tpu as pltpu
from jax.sharding import PartitionSpec as P

BF = jnp.bfloat16
F32 = jnp.float32
CAP = 48
SLOTS = 16
ROWS = CAP * SLOTS
UNIT = 2
UROWS = UNIT * CAP
UNITS = SLOTS // UNIT
CHUNK = 256
CHUNKS = ROWS // CHUNK
BACK = (0, 5, 10, SLOTS)
MESH = pl.DeviceIdType.MESH


def nt(a, b):
    return lax.dot_general(a, b, (((1,), (1,)), ((), ())), preferred_element_type=F32)


def tn(a, b):
    return lax.dot_general(a, b, (((0,), (0,)), ((), ())), preferred_element_type=F32)


def nn(a, b):
    return jnp.dot(a, b, preferred_element_type=F32)


def expert_kernel(
    tokens, gout, ids_h, probs_h, wg_h, wu_h, wd_h,
    gt_out, gg_h, gu_h, gd_h,
    xg, snd, raw, tok_v, gout_v, ids, probs, wg, wu, wd, place, pw,
    hid, gpg, gpu, acc_g, acc_u, acc_h,
    part, from_sib, from_y, snd_back, back, tail_snd, tail_rcv,
    sem_in, sem_w, sem_raw, sem_self, sem_send, sem_recv, sem_fsend, sem_yget, sem_sget,
    sem_psend, sem_precv, sem_ysend, sem_yrecv, sem_bself, sem_bsend, sem_brecv, sem_tail,
):
    ep = lax.axis_index("ep")
    t = lax.axis_index("etp")
    z, x = ep // 4, ep % 4
    y, core = t // 2, t % 2
    width = tokens.shape[1]
    t_up, t_down, t_far = (t + 2) % 8, (t + 6) % 8, (t + 4) % 8
    t_sib = t + 1 - 2 * core

    def target(j):
        i = j % 4
        return ((z + i) % 4) * 4 + (x + i + j // 4) % 4

    def source(j):
        i = j % 4
        return ((z + 4 - i) % 4) * 4 + (x + 8 - i - j // 4) % 4

    def cols(f):
        return pl.ds(pl.multiple_of(f * width, 128), width)

    def slot(j):
        return pl.ds(pl.multiple_of(j * CAP, 16), CAP)

    def remote(src, dst, ss, rs, e, f):
        return pltpu.make_async_remote_copy(
            src_ref=src, dst_ref=dst, send_sem=ss, recv_sem=rs,
            device_id={"ep": e, "etp": f}, device_id_type=MESH,
        )

    w_copies = [
        pltpu.make_async_copy(h.at[0], v, sem_w.at[i])
        for i, (h, v) in enumerate(((wg_h, wg), (wu_h, wu), (wd_h, wd)))
    ]
    in_copies = [
        pltpu.make_async_copy(h, v, sem_in.at[i])
        for i, (h, v) in enumerate(((tokens, tok_v), (gout, gout_v), (ids_h, ids), (probs_h, probs)))
    ]
    for i in (2, 3, 0, 1):
        in_copies[i].start()

    barrier = pltpu.get_barrier_semaphore()

    @pl.loop(1, SLOTS)
    def _(j):
        pl.semaphore_signal(barrier, inc=1, device_id={"ep": target(j), "etp": t}, device_id_type=MESH)

    for f in (t_up, t_down, t_far, t_sib):
        pl.semaphore_signal(barrier, inc=1, device_id={"ep": ep, "etp": f}, device_id_type=MESH)

    for copy in w_copies:
        copy.start()
    in_copies[2].wait()
    in_copies[3].wait()

    lane = lax.broadcasted_iota(jnp.int32, (128, 128), 1)
    row = lax.broadcasted_iota(jnp.int32, (128, 128), 0)
    j = lax.broadcasted_iota(jnp.int32, (SLOTS, 128), 0)
    ji = j & 3
    expert = ((z + ji) & 3) * 4 + ((x + ji + (j >> 2)) & 3)
    hit = jnp.zeros((SLOTS, 128), F32)
    weight = jnp.zeros((SLOTS, 128), F32)
    for k in range(ids.shape[0]):
        same = ids[k : k + 1, :] == expert
        hit = hit + jnp.where(same, 1.0, 0.0)
        weight = weight + jnp.where(same, probs[k : k + 1, :], 0.0)
    earlier = jnp.where(row < lane, 1.0, 0.0).astype(BF)
    pos = nn(hit.astype(BF), earlier)
    rank = lax.broadcasted_iota(jnp.int32, (CAP, 128), 0).astype(F32)
    for j in range(SLOTS):
        one = jnp.where(pos[j : j + 1] == rank, hit[j : j + 1], 0.0)
        place[j * CAP : (j + 1) * CAP, :] = one.astype(BF)
        pw[j * CAP : (j + 1) * CAP, :] = jnp.broadcast_to(
            jnp.sum(one * weight[j : j + 1], axis=1, keepdims=True), (CAP, 128)
        )

    raw_copies = [
        remote(src, raw.at[i], sem_raw.at[0, i], sem_raw.at[1, i], ep, t_far)
        for i, src in enumerate((tokens, gout))
    ]

    def fill(b, g, tok, grad):
        rows = pl.ds(g * 192, 192)
        one = place[rows, :]
        snd[b, 0, rows, :] = nn(one, tok).astype(BF)
        snd[b, 1, rows, :] = (nn(one, grad) * pw[rows, 0:1]).astype(BF)

    def own_copy(b):
        f = (t, t_far)[b]
        return pltpu.make_async_copy(
            snd.at[b, :, pl.ds(0, CAP), :], xg.at[:, pl.ds(0, CAP), cols(f)], sem_self.at[b]
        )

    def out_copy(b, j, e):
        f = (t, t_far)[b]
        return remote(
            snd.at[b, :, slot(j), :], xg.at[:, slot(j), cols(f)],
            sem_send.at[b], sem_recv.at[b, j // UNIT], e, t,
        )

    def send(b, u):
        for j in range(u * UNIT, (u + 1) * UNIT):
            if j == 0:
                own_copy(b).start()
            else:
                out_copy(b, j, target(j)).start()

    def fwd_copy(kind, u):
        rows = pl.ds(u * UROWS, UROWS)
        f = (t, t, t, t_far, t_down, t_up)[kind]
        to = (t_up, t_down, t_sib, t_sib, t_sib, t_sib)[kind]
        ref = xg.at[:, rows, cols(f)]
        if kind < 2:
            return remote(ref, ref, sem_fsend.at[0], sem_yget.at[kind, u], ep, to)
        return remote(ref, ref, sem_fsend.at[1], sem_sget.at[min(u // 3, 2)], ep, to)

    def got(b, u):
        first = max(1, u * UNIT)
        rows = pl.ds(first * CAP, ((u + 1) * UNIT - first) * CAP)
        if u == 0:
            own_copy(b).wait()
        ref = xg.at[:, rows, cols((t, t_far)[b])]
        remote(ref, ref, sem_send.at[b], sem_recv.at[b, u], ep, t_sib).wait_recv()

    def fwd_a(u):
        got(0, u)
        for kind in (0, 1, 2):
            fwd_copy(kind, u).start()

    def fwd_b(u):
        got(1, u)
        fwd_copy(3, u).start()

    def fwd_y(u):
        rows = pl.ds(u * UROWS, UROWS)
        for kind in (0, 1):
            ref = xg.at[:, rows, cols((t_down, t_up)[kind])]
            remote(ref, ref, sem_fsend.at[0], sem_yget.at[kind, u], ep, t_sib).wait_recv()
            fwd_copy(4 + kind, u).start()

    def whole(c):
        first, last = ((0, 3), (3, 6), (6, 8))[c]
        ref = xg.at[:, pl.ds(first * UROWS, (last - first) * UROWS), pl.ds(0, 4 * width)]
        remote(ref, ref, sem_fsend.at[1], sem_sget.at[c], ep, t_sib).wait_recv()

    in_copies[0].wait()
    in_copies[1].wait()
    fill(0, 0, tok_v[...], gout_v[...])
    pl.semaphore_wait(barrier, SLOTS - 1 + 4)
    for copy in raw_copies:
        copy.start()
    send(0, 0)
    send(0, 1)
    fill(0, 1, tok_v[...], gout_v[...])
    send(0, 2)
    send(0, 3)
    fill(0, 2, tok_v[...], gout_v[...])
    fill(0, 3, tok_v[...], gout_v[...])
    fwd_a(0)
    fwd_a(1)
    for copy in raw_copies:
        copy.wait_recv()
    fill(1, 0, raw[0], raw[1])
    send(1, 0)
    send(1, 1)
    fill(1, 1, raw[0], raw[1])
    send(1, 2)
    fwd_a(2)
    send(0, 4)
    send(0, 5)
    send(1, 3)
    fill(1, 2, raw[0], raw[1])
    send(1, 4)
    send(1, 5)
    fill(1, 3, raw[0], raw[1])
    send(0, 6)
    send(0, 7)
    send(1, 6)
    send(1, 7)

    def tiles(n, body, services=None):
        services = services or {}

        @pl.loop(0, n)
        def _(k):
            body(k)
            for at, calls in services.items():
                @pl.when(k == at)
                def _():
                    for call in calls:
                        call()

    def forward(c, services):
        rows = pl.ds(c * CHUNK, CHUNK)
        for acc, side, w, calls in ((acc_g, 0, wg, services[0]), (acc_u, 0, wu, services[1]), (acc_h, 1, wd, services[2])):
            acc[...] = nt(xg[side, rows, :], w[...])
            for call in calls:
                call()
        piece = 64

        @pl.loop(0, CHUNK // piece)
        def _(i):
            rs = pl.ds(pl.multiple_of(i * piece, piece), piece)
            rd = pl.ds(pl.multiple_of(c * CHUNK + i * piece, piece), piece)
            g = acc_g[rs, :]
            u = acc_u[rs, :]
            h = acc_h[rs, :]
            s = jax.nn.sigmoid(g)
            sg = g * s
            hid[rd, :] = (sg * u).astype(BF)
            gpg[rd, :] = (h * u * s * (1.0 + g * (1.0 - s))).astype(BF)
            gpu[rd, :] = (h * sg).astype(BF)

    steps = (1, 3, 2, 0)

    def chunk_rows(c):
        return pl.ds(c * CHUNK, CHUNK)

    def sib_copy(c, i):
        rows = chunk_rows(c)
        return remote(
            part.at[i, 1 - core, rows, :], from_sib.at[i, rows, :],
            sem_psend.at[0], sem_precv.at[c, i], ep, t_sib,
        )

    def y_copy(c, i):
        rows = chunk_rows(c)
        return remote(
            part.at[i, core, rows, :], from_y.at[i, rows, :],
            sem_ysend.at[0], sem_yrecv.at[c, i], ep, (t_up, t_down)[i],
        )

    def quarter(c, i):
        rows = chunk_rows(c)
        q = (y + steps[i]) % 4
        ws = pl.ds(pl.multiple_of(q * 2 * width, 128), 2 * width)
        p = nn(gpg[rows, :], wg[:, ws]) + nn(gpu[rows, :], wu[:, ws])
        part[i, 0, rows, :] = p[:, :width].astype(BF)
        part[i, 1, rows, :] = p[:, width:].astype(BF)
        sib_copy(c, i).start()

    def pair(c, i):
        rows = chunk_rows(c)
        sib_copy(c, i).wait_recv()
        return part[i, core, rows, :].astype(F32) + from_sib[i, rows, :].astype(F32)

    def pair_y(c, i):
        part[i, core, chunk_rows(c), :] = pair(c, i).astype(BF)
        y_copy(c, i).start()

    def back_copy(b, j, e):
        return remote(
            snd_back.at[b, slot(j), :], back.at[b, slot(j), :],
            sem_bsend.at[0], sem_brecv.at[b], e, t,
        )

    def own_back(b):
        return pltpu.make_async_copy(
            snd_back.at[b, pl.ds(0, CAP), :], back.at[b, pl.ds(0, CAP), :], sem_bself.at[b]
        )

    def send_back(c, b):
        for j in range(BACK[c], BACK[c + 1]):
            if j == 0:
                own_back(b).start()
            else:
                back_copy(b, j, source(j)).start()

    def pair_far(c):
        snd_back[1, chunk_rows(c), :] = pair(c, 2).astype(BF)
        send_back(c, 1)

    def pair_own(c):
        rows = chunk_rows(c)
        mine = pair(c, 3)
        for i in (0, 1):
            y_copy(c, i).wait_recv()
            mine = mine + from_y[i, rows, :].astype(F32)
        snd_back[0, rows, :] = mine.astype(BF)
        send_back(c, 0)

    tail = remote(tail_snd, tail_rcv, sem_tail.at[0], sem_tail.at[1], ep, t_far)

    others = pl.ds(CAP, ROWS - CAP)

    def got_back(b):
        own_back(b).wait()
        remote(
            snd_back.at[b, others, :], back.at[b, others, :], sem_bsend.at[0], sem_brecv.at[b], ep, t_sib
        ).wait_recv()

    def combine_far():
        got_back(1)
        tail_snd[...] = tn(place[...], back[1]).astype(BF)
        tail.start()

    def combine_own():
        got_back(0)
        mine = tn(place[...], back[0])
        tail.wait_recv()
        gt_out[...] = (mine + tail_rcv[...].astype(F32)).astype(BF)

    wt = 1024

    def grad_tile(i, k):
        ks = pl.ds(pl.multiple_of(k * wt, wt), wt)
        (gd_h, gg_h, gu_h)[i][0, :, ks] = tn((hid, gpg, gpu)[i][...], xg[(1, 0, 0)[i], :, ks]).astype(BF)

    nw = xg.shape[2] // wt

    def act(f, *args):
        return lambda: f(*args)

    def back_part(c, calls):
        quarter(c, 0)
        quarter(c, 1)
        pair_y(c, 0)
        for call in calls[0]:
            call()
        quarter(c, 2)
        pair_y(c, 1)
        for call in calls[1]:
            call()
        quarter(c, 3)
        pair_far(c)
        for call in calls[2]:
            call()

    fwd_a(3)
    fwd_y(0)
    fwd_b(0)
    fwd_b(1)
    fwd_y(1)
    fwd_b(2)
    fwd_a(4)
    fwd_y(2)
    for copy in w_copies:
        copy.wait()
    whole(0)
    forward(0, ([act(fwd_a, 5), act(fwd_y, 3)], [act(fwd_b, 3)], [act(fwd_b, 4), act(fwd_y, 4)]))
    back_part(0, ([act(fwd_a, 6), act(fwd_b, 5)], [act(fwd_a, 7)], []))
    fwd_y(5)
    whole(1)
    forward(1, ([], [act(fwd_b, 6)], [act(fwd_y, 6)]))
    back_part(1, ([act(fwd_b, 7)], [], []))
    fwd_y(7)
    whole(2)
    forward(2, ([act(pair_own, 0)], [], [act(pair_own, 1)]))
    back_part(2, ([], [], []))
    tiles(nw, lambda k: grad_tile(0, k), {1: [act(pair_own, 2)]})
    tiles(nw, lambda k: grad_tile(1, k), {0: [combine_far]})
    tiles(nw, lambda k: grad_tile(2, k), {1: [combine_own]})

    for copy in raw_copies:
        copy.wait_send()
    tail.wait_send()
    for b in (0, 1):
        remote(
            snd.at[b, :, others, :], xg.at[:, others, pl.ds(0, width)], sem_send.at[b], sem_recv.at[b, 0], ep, t_sib
        ).wait_send()
    ref = xg.at[:, :, pl.ds(0, 2 * width)]
    remote(ref, ref, sem_fsend.at[0], sem_sget.at[0], ep, t_sib).wait_send()
    ref = xg.at[:, :, pl.ds(0, 4 * width)]
    remote(ref, ref, sem_fsend.at[1], sem_sget.at[0], ep, t_sib).wait_send()
    remote(from_sib, from_sib, sem_psend.at[0], sem_precv.at[0, 0], ep, t_sib).wait_send()
    remote(from_y, from_y, sem_ysend.at[0], sem_yrecv.at[0, 0], ep, t_sib).wait_send()
    ref = snd_back.at[:, others, :]
    remote(ref, ref, sem_bsend.at[0], sem_brecv.at[0], ep, t_sib).wait_send()


def local(tokens, grad_out, probs, expert_ids, w_gate, w_up, w_down):
    toks, width = tokens.shape
    _, d, ff = w_gate.shape
    w_gate = w_gate.transpose(0, 2, 1)
    w_up = w_up.transpose(0, 2, 1)
    vmem = pl.BlockSpec(memory_space=pltpu.VMEM)
    hbm = pl.BlockSpec(memory_space=pl.ANY)
    dma = pltpu.SemaphoreType.DMA
    n = CHUNK
    gt, gg, gu, gd = pl.pallas_call(
        expert_kernel,
        out_shape=[
            jax.ShapeDtypeStruct((toks, width), BF),
            pltpu.VMEM(w_gate.shape, BF),
            pltpu.VMEM(w_up.shape, BF),
            pltpu.VMEM(w_down.shape, BF),
        ],
        in_specs=[hbm] * 7,
        out_specs=[vmem] * 4,
        scratch_shapes=[
            pltpu.VMEM((2, ROWS, d), BF),
            pltpu.VMEM((2, 2, ROWS, width), BF),
            pltpu.VMEM((2, toks, width), BF),
            pltpu.VMEM((toks, width), BF),
            pltpu.VMEM((toks, width), BF),
            pltpu.VMEM(expert_ids.T.shape, jnp.int32),
            pltpu.VMEM(probs.T.shape, F32),
            pltpu.VMEM((ff, d), BF),
            pltpu.VMEM((ff, d), BF),
            pltpu.VMEM((ff, d), BF),
            pltpu.VMEM((ROWS, toks), BF),
            pltpu.VMEM((ROWS, 128), F32),
            pltpu.VMEM((ROWS, ff), BF),
            pltpu.VMEM((ROWS, ff), BF),
            pltpu.VMEM((ROWS, ff), BF),
            pltpu.VMEM((n, ff), F32),
            pltpu.VMEM((n, ff), F32),
            pltpu.VMEM((n, ff), F32),
            pltpu.VMEM((4, 2, ROWS, width), BF),
            pltpu.VMEM((4, ROWS, width), BF),
            pltpu.VMEM((2, ROWS, width), BF),
            pltpu.VMEM((2, ROWS, width), BF),
            pltpu.VMEM((2, ROWS, width), BF),
            pltpu.VMEM((toks, width), BF),
            pltpu.VMEM((toks, width), BF),
            dma((4,)),
            dma((3,)),
            dma((2, 2)),
            dma((2,)),
            dma((2,)),
            dma((2, UNITS)),
            dma((2,)),
            dma((2, UNITS)),
            dma((CHUNKS,)),
            dma((1,)),
            dma((CHUNKS, 4)),
            dma((1,)),
            dma((CHUNKS, 2)),
            dma((2,)),
            dma((1,)),
            dma((2,)),
            dma((2,)),
        ],
        compiler_params=pltpu.CompilerParams(
            collective_id=0, has_side_effects=True, vmem_limit_bytes=46 * 2**20
        ),
    )(tokens, grad_out, expert_ids.T, probs.T, w_gate, w_up, w_down)
    return gt, gg.transpose(0, 2, 1), gu.transpose(0, 2, 1), gd


def solution(mesh):
    return jax.shard_map(
        local,
        mesh=mesh,
        in_specs=(
            P("ep", "etp"),
            P("ep", "etp"),
            P("ep", None),
            P("ep", None),
            P("ep", None, "etp"),
            P("ep", None, "etp"),
            P("ep", "etp", None),
        ),
        out_specs=(
            P("ep", "etp"),
            P("ep", None, "etp"),
            P("ep", None, "etp"),
            P("ep", "etp", None),
        ),
        check_vma=False,
    )
```

time: 136 us -> 89.5 us (0.66)
  local copies, waits for them, and re-layouts: 33.7 us -> 6.61 us
  Pallas kernels: 100 us -> 81.1 us
    pallas_call x1, Pallas kernels: 100 us -> 81.1 us  [local(): pl.pallas_call(expert_kernel, out_shape=[jax.ShapeDtypeStruct((toks, widt...]
    unnamed x8 -> x6, local copies, waits for them, and re-layouts: 20.9 us -> 6.61 us
    pallas_call x2 -> x0, local copies, waits for them, and re-layouts: 12.9 us -> none  [local(): pl.pallas_call(expert_kernel, out_shape=[jax.ShapeDtypeStruct((toks, widt...]
where the time goes in v1:
time: 89.5 us; the launch traced here: 88.4 us
  Pallas kernels  81.1 us (91%)
  local copies, waits for them, and re-layouts  6.61 us (7%)
    pallas_call x1, Pallas kernels, local(): pl.pallas_call(expert_kernel, out_shape=[jax.ShapeDtypeStruct((toks, widt...  81.1 us
    unnamed x6, local copies, waits for them, and re-layouts  6.61 us

profile of v1, /device:TPU:0, one launch (start us, length us, event | category | flops | bytes accessed | tf_op | source)
XLA Modules:
  0.0 88.4 jit_solution(4064393965034835818)
XLA Ops:
  0.6 81.1 %shard_map.102 = (bf16[128,384]{1,0:T(8,128)(2,1)}, bf16[1,672,3072]{2,1,0:T(8,128)(2,1)S(1)}, bf16[1,672,3072]{2,1,0:T(8,128)(2,1)S(1)}, bf16[1,672,3072]{2,1,0:T(8,128)(2,1)S(1)}) custom-call(bf16[128,384]{1,0:T(8,128)(2,1)} %tokens.1, bf16[128,384]{1,0:T(8,128)(2,1)} %gout.1, s32[4,128]{1,0:T(4,128)} %bitcast.10, f32[4,128]{1,0:T(4,128)} %bitcast.11, ...), custom_call_target="tpu_custom_call" | custom-call | tf_op jit(solution)/shard_map/pallas_call | solution.py:421
  81.8 2.0 %copy.15 = bf16[1,3072,672]{1,2,0:T(8,128)(2,1)} copy(bf16[1,3072,672]{1,2,0:T(8,128)(2,1)S(1)} %bitcast.7) | data formatting | bytes 8257536
  83.7 2.0 %copy.16 = bf16[1,3072,672]{1,2,0:T(8,128)(2,1)} copy(bf16[1,3072,672]{1,2,0:T(8,128)(2,1)S(1)} %bitcast.6) | data formatting | bytes 8257536
  85.7 0.0 copy-start
  85.7 2.0 %copy.17 = bf16[1,672,3072]{2,1,0:T(8,128)(2,1)} copy(bf16[1,672,3072]{2,1,0:T(8,128)(2,1)S(1)} %get-tuple-element.15) | data formatting | bytes 8257536
  87.7 0.0 copy-done
  87.7 0.6 copy.18
Async XLA Ops:
  85.7 2.0 %copy-start = (bf16[128,384]{1,0:T(8,128)(2,1)S(1)}, bf16[128,384]{1,0:T(8,128)(2,1)}, u32[]{:S(2)}) copy-start(bf16[128,384]{1,0:T(8,128)(2,1)} %get-tuple-element.20) | copy-start | bytes 294916

commit v2 on v1

--- a/solution.py
+++ b/solution.py
@@ -14,9 +14,9 @@
 UNIT = 2
 UROWS = UNIT * CAP
 UNITS = SLOTS // UNIT
-CHUNK = 256
-CHUNKS = ROWS // CHUNK
-BACK = (0, 5, 10, SLOTS)
+EDGES = (0, 192, 480, ROWS)
+CHUNKS = len(EDGES) - 1
+BACK = (0, 4, 10, SLOTS)
 MESH = pl.DeviceIdType.MESH
 
 
@@ -153,7 +153,7 @@
         ref = xg.at[:, rows, cols(f)]
         if kind < 2:
             return remote(ref, ref, sem_fsend.at[0], sem_yget.at[kind, u], ep, to)
-        return remote(ref, ref, sem_fsend.at[1], sem_sget.at[min(u // 3, 2)], ep, to)
+        return remote(ref, ref, sem_fsend.at[1], sem_sget.at[(u + 1) // 3], ep, to)
 
     def got(b, u):
         first = max(1, u * UNIT)
@@ -180,8 +180,7 @@
             fwd_copy(4 + kind, u).start()
 
     def whole(c):
-        first, last = ((0, 3), (3, 6), (6, 8))[c]
-        ref = xg.at[:, pl.ds(first * UROWS, (last - first) * UROWS), pl.ds(0, 4 * width)]
+        ref = xg.at[:, pl.ds(EDGES[c], EDGES[c + 1] - EDGES[c]), pl.ds(0, 4 * width)]
         remote(ref, ref, sem_fsend.at[1], sem_sget.at[c], ep, t_sib).wait_recv()
 
     in_copies[0].wait()
@@ -204,18 +203,18 @@
     fill(1, 0, raw[0], raw[1])
     send(1, 0)
     send(1, 1)
+    send(0, 4)
+    fwd_a(2)
     fill(1, 1, raw[0], raw[1])
     send(1, 2)
-    fwd_a(2)
-    send(0, 4)
     send(0, 5)
     send(1, 3)
+    send(0, 6)
     fill(1, 2, raw[0], raw[1])
     send(1, 4)
+    send(0, 7)
     send(1, 5)
     fill(1, 3, raw[0], raw[1])
-    send(0, 6)
-    send(0, 7)
     send(1, 6)
     send(1, 7)
 
@@ -232,17 +231,17 @@
                         call()
 
     def forward(c, services):
-        rows = pl.ds(c * CHUNK, CHUNK)
+        rows = pl.ds(EDGES[c], EDGES[c + 1] - EDGES[c])
         for acc, side, w, calls in ((acc_g, 0, wg, services[0]), (acc_u, 0, wu, services[1]), (acc_h, 1, wd, services[2])):
-            acc[...] = nt(xg[side, rows, :], w[...])
+            acc[0 : EDGES[c + 1] - EDGES[c], :] = nt(xg[side, rows, :], w[...])
             for call in calls:
                 call()
-        piece = 64
-
-        @pl.loop(0, CHUNK // piece)
+        piece = 96
+
+        @pl.loop(0, (EDGES[c + 1] - EDGES[c]) // piece)
         def _(i):
             rs = pl.ds(pl.multiple_of(i * piece, piece), piece)
-            rd = pl.ds(pl.multiple_of(c * CHUNK + i * piece, piece), piece)
+            rd = pl.ds(pl.multiple_of(EDGES[c] + i * piece, piece), piece)
             g = acc_g[rs, :]
             u = acc_u[rs, :]
             h = acc_h[rs, :]
@@ -255,7 +254,7 @@
     steps = (1, 3, 2, 0)
 
     def chunk_rows(c):
-        return pl.ds(c * CHUNK, CHUNK)
+        return pl.ds(EDGES[c], EDGES[c + 1] - EDGES[c])
 
     def sib_copy(c, i):
         rows = chunk_rows(c)
@@ -352,14 +351,16 @@
     def act(f, *args):
         return lambda: f(*args)
 
-    def back_part(c, calls):
+    def back_part(c, calls, hold=False):
         quarter(c, 0)
         quarter(c, 1)
-        pair_y(c, 0)
+        if not hold:
+            pair_y(c, 0)
         for call in calls[0]:
             call()
         quarter(c, 2)
-        pair_y(c, 1)
+        if not hold:
+            pair_y(c, 1)
         for call in calls[1]:
             call()
         quarter(c, 3)
@@ -372,22 +373,20 @@
     fwd_b(0)
     fwd_b(1)
     fwd_y(1)
-    fwd_b(2)
-    fwd_a(4)
-    fwd_y(2)
     for copy in w_copies:
         copy.wait()
     whole(0)
-    forward(0, ([act(fwd_a, 5), act(fwd_y, 3)], [act(fwd_b, 3)], [act(fwd_b, 4), act(fwd_y, 4)]))
-    back_part(0, ([act(fwd_a, 6), act(fwd_b, 5)], [act(fwd_a, 7)], []))
-    fwd_y(5)
+    forward(0, ([act(fwd_a, 4)], [act(fwd_y, 2), act(fwd_b, 2)], [act(fwd_a, 5)]))
+    back_part(0, ([act(fwd_b, 3), act(fwd_y, 3)], [act(fwd_a, 6)], []), hold=True)
+    fwd_b(4)
+    fwd_y(4)
     whole(1)
-    forward(1, ([], [act(fwd_b, 6)], [act(fwd_y, 6)]))
-    back_part(1, ([act(fwd_b, 7)], [], []))
+    forward(1, ([act(fwd_a, 7)], [act(fwd_b, 5), act(fwd_y, 5)], [act(pair_y, 0, 0), act(pair_y, 0, 1)]))
+    back_part(1, ([act(fwd_b, 6), act(fwd_y, 6)], [], [act(fwd_b, 7)]))
     fwd_y(7)
     whole(2)
-    forward(2, ([act(pair_own, 0)], [], [act(pair_own, 1)]))
-    back_part(2, ([], [], []))
+    forward(2, ([], [], [act(pair_own, 0)]))
+    back_part(2, ([], [], [act(pair_own, 1)]))
     tiles(nw, lambda k: grad_tile(0, k), {1: [act(pair_own, 2)]})
     tiles(nw, lambda k: grad_tile(1, k), {0: [combine_far]})
     tiles(nw, lambda k: grad_tile(2, k), {1: [combine_own]})
@@ -409,6 +408,15 @@
     remote(ref, ref, sem_bsend.at[0], sem_brecv.at[0], ep, t_sib).wait_send()
 
 
+def leave_kernel(*refs):
+    n = len(refs) // 2
+    copies = [pltpu.make_async_copy(refs[i], refs[n + i], refs[-1].at[i]) for i in range(n)]
+    for copy in copies:
+        copy.start()
+    for copy in copies:
+        copy.wait()
+
+
 def local(tokens, grad_out, probs, expert_ids, w_gate, w_up, w_down):
     toks, width = tokens.shape
     _, d, ff = w_gate.shape
@@ -417,11 +425,11 @@
     vmem = pl.BlockSpec(memory_space=pltpu.VMEM)
     hbm = pl.BlockSpec(memory_space=pl.ANY)
     dma = pltpu.SemaphoreType.DMA
-    n = CHUNK
-    gt, gg, gu, gd = pl.pallas_call(
+    n = max(b - a for a, b in zip(EDGES, EDGES[1:]))
+    results = pl.pallas_call(
         expert_kernel,
         out_shape=[
-            jax.ShapeDtypeStruct((toks, width), BF),
+            pltpu.VMEM((toks, width), BF),
             pltpu.VMEM(w_gate.shape, BF),
             pltpu.VMEM(w_up.shape, BF),
             pltpu.VMEM(w_down.shape, BF),
@@ -476,6 +484,14 @@
             collective_id=0, has_side_effects=True, vmem_limit_bytes=46 * 2**20
         ),
     )(tokens, grad_out, expert_ids.T, probs.T, w_gate, w_up, w_down)
+    gt, gg, gu, gd = pl.pallas_call(
+        leave_kernel,
+        out_shape=[jax.ShapeDtypeStruct(r.shape, r.dtype) for r in results],
+        in_specs=[hbm] * 4,
+        out_specs=[hbm] * 4,
+        scratch_shapes=[dma((4,))],
+        compiler_params=pltpu.CompilerParams(vmem_limit_bytes=2**20),
+    )(*results)
     return gt, gg.transpose(0, 2, 1), gu.transpose(0, 2, 1), gd
 
 

time: 89.5 us -> 85.6 us (0.956)
  local copies, waits for them, and re-layouts: 6.61 us -> 0 us
  Pallas kernels: 81.1 us -> 84 us
    unnamed x6 -> x0, local copies, waits for them, and re-layouts: 6.61 us -> none
    pallas_call x1 -> x2, Pallas kernels: 81.1 us -> 84 us  [the longest x1 79.4 us: local(): pl.pallas_call(expert_kernel, out_shape=[pltpu.VMEM((toks, width), BF), p...]
where the time goes in v2:
time: 85.6 us; the launch traced here: 84.9 us
  Pallas kernels  84 us (98%)
    pallas_call x1, Pallas kernels, local(): pl.pallas_call(expert_kernel, out_shape=[pltpu.VMEM((toks, width), BF), p...  79.4 us
    pallas_call x1, Pallas kernels, local(): pl.pallas_call(leave_kernel, out_shape=[jax.ShapeDtypeStruct(r.shape, r.d...  4.66 us

profile of v2, /device:TPU:0, one launch (start us, length us, event | category | flops | bytes accessed | tf_op | source)
XLA Modules:
  0.0 84.9 jit_solution(12161394375407132619)
XLA Ops:
  0.6 79.4 %shard_map.102 = (bf16[128,384]{1,0:T(8,128)(2,1)S(1)}, bf16[1,672,3072]{2,1,0:T(8,128)(2,1)S(1)}, bf16[1,672,3072]{2,1,0:T(8,128)(2,1)S(1)}, bf16[1,672,3072]{2,1,0:T(8,128)(2,1)S(1)}) custom-call(bf16[128,384]{1,0:T(8,128)(2,1)} %tokens.1, bf16[128,384]{1,0:T(8,128)(2,1)} %gout.1, s32[4,128]{1,0:T(4,128)} %bitcast.8, f32[4,128]{1,0:T(4,128)} %bitcast.9, ...), custom_call_target="tpu_custom_call" | custom-call | tf_op jit(solution)/shard_map/pallas_call | solution.py:429
  80.0 4.7 %shard_map.103 = (bf16[128,384]{1,0:T(8,128)(2,1)}, bf16[1,672,3072]{2,1,0:T(8,128)(2,1)}, bf16[1,672,3072]{2,1,0:T(8,128)(2,1)}, bf16[1,672,3072]{2,1,0:T(8,128)(2,1)}) custom-call(bf16[128,384]{1,0:T(8,128)(2,1)S(1)} %get-tuple-element.12.refs_0_, bf16[1,672,3072]{2,1,0:T(8,128)(2,1)S(1)} %get-tuple-element.13.refs_1_, ...), custom_call_target="tpu_custom_call" | custom-call | tf_op jit(solution)/shard_map/pallas_call | solution.py:487
